TPU v7x, 512 devices: a whole 4x4x16 slice. The times are simulated.
512 devices in a mesh: ctx: 128 (over x, z, core), head: 4 (over y).
Axes of the slice: x: 4, y: 4, z: 16, core: 2. Of those that a mesh axis runs over, the one named last changes fastest.
Arguments:
- query: bfloat16 [65536, 1024], P('ctx', 'head'), may hold values from -7.5 to 7.5
- key: bfloat16 [65536, 1024], P('ctx', 'head'), may hold values from -7.5 to 7.5
- value: bfloat16 [65536, 1024], P('ctx', 'head'), may hold values from -6 to 6
- grad_out: bfloat16 [65536, 1024], P('ctx', 'head'), may hold values from -6 to 6
- picks: int32 [512, 16, 4], P('ctx', 'head'), may hold values from 0 to 127, as said below
Outputs:
- attn_out: bfloat16 [65536, 1024], P('ctx', 'head')
- grad_query: bfloat16 [65536, 1024], P('ctx', 'head')
- grad_key: bfloat16 [65536, 1024], P('ctx', 'head')
- grad_value: bfloat16 [65536, 1024], P('ctx', 'head')
Inputs may be any that keep to these rules, and one draw needn't show every extreme that they name: picks[g, h, 0] is the block that holds tile g; every other entry is that block again (no further block) or an earlier block. Among the tiles of one block and one group of 4 consecutive heads, no earlier block is named twice.
All inputs are finite; a program needn't handle non-finite values.
Results may differ from a plain program's by a relative error of at most 0.017.
Values may be sent and summed in bfloat16 or wider, within the bound.
A program may use at most 64 MiB of HBM per device.

v0:
```python
import math

import jax
import jax.numpy as jnp
from jax import lax
from jax.sharding import PartitionSpec as P

masked_value = -1e30
highest = lax.Precision.HIGHEST


def attend_slots(q_slots, head_ids, k_heads, v_heads, scaling):
    key_rows = jnp.take(k_heads, head_ids, axis=0)
    value_rows = jnp.take(v_heads, head_ids, axis=0)
    scores = (
        jnp.einsum("ndq,nkd->nqk", q_slots, key_rows, preferred_element_type=jnp.float32) * scaling
    )
    peak_score = jnp.max(scores, axis=-1, keepdims=True)
    log_total = peak_score + jnp.log(jnp.sum(jnp.exp(scores - peak_score), axis=-1, keepdims=True))
    attend_low = jnp.exp(scores - log_total).astype(jnp.bfloat16)
    outputs = jnp.einsum("nqk,nkd->ndq", attend_low, value_rows, preferred_element_type=jnp.float32)
    return (outputs, log_total[..., 0])


def slot_grads(q_slots, g_slots, c_slots, lse_slots, head_ids, k_heads, v_heads, scaling):
    key_rows = jnp.take(k_heads, head_ids, axis=0)
    value_rows = jnp.take(v_heads, head_ids, axis=0)
    scores = (
        jnp.einsum("ndq,nkd->nqk", q_slots, key_rows, preferred_element_type=jnp.float32) * scaling
    )
    attend = jnp.exp(scores - lse_slots[..., None])
    attend_low = attend.astype(jnp.bfloat16)
    grad_v = jnp.einsum("nqk,ndq->nkd", attend_low, g_slots, preferred_element_type=jnp.float32)
    grad_prob = jnp.einsum("ndq,nkd->nqk", g_slots, value_rows, preferred_element_type=jnp.float32)
    dscore = (attend * (grad_prob - c_slots[..., None])).astype(jnp.bfloat16)
    grad_k = (
        jnp.einsum("nqk,ndq->nkd", dscore, q_slots, preferred_element_type=jnp.float32) * scaling
    )
    grad_q = (
        jnp.einsum("nqk,nkd->ndq", dscore, key_rows, preferred_element_type=jnp.float32) * scaling
    )
    return (grad_k, grad_v, grad_q)


def local(query, key, value, grad_out, picks):
    row_count, columns = query.shape
    tiles_dev, groups, picked = picks.shape
    head_dim = columns // groups
    tile_rows = row_count // tiles_dev
    others = picked - 1
    scaling = 1.0 / math.sqrt(head_dim)
    devices = lax.axis_size("ctx")
    own_block = lax.axis_index("ctx")
    per_group = min(8, devices)
    all_picks = lax.all_gather(picks, "ctx", axis=0, tiled=True)
    q_heads = query.reshape(row_count, groups, head_dim).transpose(1, 0, 2)
    k_heads = key.reshape(row_count, groups, head_dim).transpose(1, 0, 2)
    v_heads = value.reshape(row_count, groups, head_dim).transpose(1, 0, 2)
    q_tiles = query.reshape(tiles_dev, tile_rows, groups, head_dim)
    do_tiles = grad_out.reshape(tiles_dev, tile_rows, groups, head_dim)
    do_major = do_tiles.transpose(0, 2, 1, 3)
    positions = jnp.arange(row_count, dtype=jnp.int32)
    tile_masks = []
    for tile_step in range(tiles_dev):
        span = (tile_step + 1) * tile_rows
        query_pos = positions[tile_step * tile_rows : span]
        tile_masks.append(positions[None, :span] <= query_pos[:, None])
    targets = picks[:, :, 1:]
    active = targets != own_block
    lookup = jnp.where(active, targets, own_block).reshape(-1)
    peer_ids = jnp.arange(devices, dtype=jnp.int32)
    routing = ((targets[None] == peer_ids[:, None, None, None]) & active[None]).astype(jnp.float32)
    routing_low = routing.astype(jnp.bfloat16)
    send_q = jnp.einsum(
        "jtgi,tqgd->jdq", routing_low, q_tiles, preferred_element_type=jnp.float32
    ).astype(jnp.bfloat16)
    recv_q = lax.all_to_all(send_q, "ctx", split_axis=0, concat_axis=0, tiled=True)

    def own_forward(inputs):
        q_head, k_head, v_head = inputs
        out_list = []
        lse_list = []
        for tile_step in range(tiles_dev):
            span = (tile_step + 1) * tile_rows
            q_part = q_head[tile_step * tile_rows : span]
            scores = (
                jnp.einsum("qd,kd->qk", q_part, k_head[:span], preferred_element_type=jnp.float32)
                * scaling
            )
            scores = jnp.where(tile_masks[tile_step], scores, masked_value)
            peak_score = jnp.max(scores, axis=-1, keepdims=True)
            log_total = peak_score + jnp.log(
                jnp.sum(jnp.exp(scores - peak_score), axis=-1, keepdims=True)
            )
            attend_low = jnp.exp(scores - log_total).astype(jnp.bfloat16)
            out_list.append(jnp.dot(attend_low, v_head[:span], preferred_element_type=jnp.float32))
            lse_list.append(log_total[:, 0])
        return (jnp.concatenate(out_list, axis=0), jnp.concatenate(lse_list, axis=0))

    own_out, own_lse = lax.map(own_forward, (q_heads, k_heads, v_heads))
    sources = all_picks.reshape(devices, tiles_dev, groups, picked)[..., 1:]
    incoming = (sources == own_block) & (peer_ids[:, None, None, None] != own_block)
    live_in = jnp.any(incoming, axis=(1, 2, 3))
    group_ids = jnp.arange(groups, dtype=jnp.int32)
    head_of = jnp.sum(jnp.where(incoming, group_ids[None, None, :, None], 0), axis=(1, 2, 3))
    ranking = jnp.argsort(jnp.where(live_in, 0, 1) * devices + peer_ids)
    inverse = jnp.argsort(ranking)
    rounds = (jnp.sum(live_in.astype(jnp.int32)) + per_group - 1) // per_group
    heads_sorted = jnp.take(head_of, ranking, axis=0)
    q_sorted = jnp.take(recv_q, ranking, axis=0)

    def forward_turn(turn, totals):
        served_out, served_lse = totals
        offset = turn * per_group
        query_part = lax.dynamic_slice_in_dim(q_sorted, offset, per_group, 0)
        head_part = lax.dynamic_slice_in_dim(heads_sorted, offset, per_group, 0)
        out_part, lse_part = attend_slots(query_part, head_part, k_heads, v_heads, scaling)
        served_out = lax.dynamic_update_slice_in_dim(served_out, out_part, offset, 0)
        served_lse = lax.dynamic_update_slice_in_dim(served_lse, lse_part, offset, 0)
        return (served_out, served_lse)

    start_fwd = (
        jnp.zeros((devices, head_dim, tile_rows), jnp.float32),
        jnp.zeros((devices, tile_rows), jnp.float32),
    )
    served_out, served_lse = lax.fori_loop(0, rounds, forward_turn, start_fwd)
    back_out, back_lse = (
        lax.all_to_all(
            jnp.take(served_out, inverse, axis=0), "ctx", split_axis=0, concat_axis=0, tiled=True
        ),
        lax.all_to_all(
            jnp.take(served_lse, inverse, axis=0), "ctx", split_axis=0, concat_axis=0, tiled=True
        ),
    )
    task_out = jnp.take(back_out, lookup, axis=0).reshape(
        tiles_dev, groups, others, head_dim, tile_rows
    )
    task_lse = jnp.take(back_lse, lookup, axis=0).reshape(tiles_dev, groups, others, tile_rows)
    own_out_t = own_out.reshape(groups, tiles_dev, tile_rows, head_dim).transpose(1, 0, 2, 3)
    own_lse_t = own_lse.reshape(groups, tiles_dev, tile_rows).transpose(1, 0, 2)
    active_rows = active[..., None]
    rem_lse = jnp.where(active_rows, task_lse, masked_value)
    ceiling = jnp.maximum(own_lse_t, jnp.max(rem_lse, axis=2))
    log_total = ceiling + jnp.log(
        jnp.exp(own_lse_t - ceiling) + jnp.sum(jnp.exp(rem_lse - ceiling[:, :, None]), axis=2)
    )
    own_weight = jnp.exp(own_lse_t - log_total)
    rem_weight = jnp.where(active_rows, jnp.exp(rem_lse - log_total[:, :, None]), 0.0)
    mixed = own_weight[..., None] * own_out_t + jnp.einsum(
        "tgiq,tgidq->tgqd", rem_weight, task_out, precision=highest
    )
    out_low = mixed.astype(jnp.bfloat16)
    attn_out = out_low.transpose(0, 2, 1, 3).reshape(row_count, columns)
    row_delta = jnp.sum(do_major.astype(jnp.float32) * out_low.astype(jnp.float32), axis=-1)
    own_scaled = (own_weight[..., None] * do_major.astype(jnp.float32)).astype(jnp.bfloat16)
    own_shift = own_weight * row_delta
    g_heads = own_scaled.transpose(1, 0, 2, 3).reshape(groups, row_count, head_dim)
    c_heads = own_shift.transpose(1, 0, 2).reshape(groups, row_count)

    def own_backward(inputs):
        q_head, k_head, v_head, g_head, c_head, lse_head = inputs
        grad_k = jnp.zeros((row_count, head_dim), jnp.float32)
        grad_v = jnp.zeros((row_count, head_dim), jnp.float32)
        dq_list = []
        for tile_step in range(tiles_dev):
            first = tile_step * tile_rows
            span = (tile_step + 1) * tile_rows
            q_part = q_head[first:span]
            g_part = g_head[first:span]
            k_part = k_head[:span]
            scores = (
                jnp.einsum("qd,kd->qk", q_part, k_part, preferred_element_type=jnp.float32)
                * scaling
            )
            scores = jnp.where(tile_masks[tile_step], scores, masked_value)
            attend = jnp.exp(scores - lse_head[first:span, None])
            attend_low = attend.astype(jnp.bfloat16)
            part_dv = jnp.einsum(
                "qk,qd->kd", attend_low, g_part, preferred_element_type=jnp.float32
            )
            grad_prob = jnp.einsum(
                "qd,kd->qk", g_part, v_head[:span], preferred_element_type=jnp.float32
            )
            dscore = (attend * (grad_prob - c_head[first:span, None])).astype(jnp.bfloat16)
            part_dk = (
                jnp.einsum("qk,qd->kd", dscore, q_part, preferred_element_type=jnp.float32)
                * scaling
            )
            dq_list.append(jnp.dot(dscore, k_part, preferred_element_type=jnp.float32) * scaling)
            padding = ((0, row_count - span), (0, 0))
            grad_k = grad_k + jnp.pad(part_dk, padding)
            grad_v = grad_v + jnp.pad(part_dv, padding)
        return (grad_k, grad_v, jnp.concatenate(dq_list, axis=0))

    own_dk, own_dv, own_dq = lax.map(
        own_backward, (q_heads, k_heads, v_heads, g_heads, c_heads, own_lse)
    )
    rem_shift = rem_weight * row_delta[:, :, None]
    rem_scaled = (rem_weight[..., None] * do_major[:, :, None].astype(jnp.float32)).astype(
        jnp.bfloat16
    )
    send_g = jnp.einsum(
        "jtgi,tgiqd->jdq", routing_low, rem_scaled, preferred_element_type=jnp.float32
    )
    send_c = jnp.einsum("jtgi,tgiq->jq", routing, rem_shift, precision=highest)
    recv_g, recv_c = (
        lax.all_to_all(send_g, "ctx", split_axis=0, concat_axis=0, tiled=True),
        lax.all_to_all(send_c, "ctx", split_axis=0, concat_axis=0, tiled=True),
    )
    g_sorted = jnp.take(recv_g, ranking, axis=0).astype(jnp.bfloat16)
    c_sorted = jnp.take(recv_c, ranking, axis=0)

    def backward_turn(turn, totals):
        grad_k, grad_v, served_dq = totals
        offset = turn * per_group
        query_part = lax.dynamic_slice_in_dim(q_sorted, offset, per_group, 0)
        cot_part = lax.dynamic_slice_in_dim(g_sorted, offset, per_group, 0)
        shift_part = lax.dynamic_slice_in_dim(c_sorted, offset, per_group, 0)
        lse_part = lax.dynamic_slice_in_dim(served_lse, offset, per_group, 0)
        head_part = lax.dynamic_slice_in_dim(heads_sorted, offset, per_group, 0)
        part_dk, part_dv, part_dq = slot_grads(
            query_part, cot_part, shift_part, lse_part, head_part, k_heads, v_heads, scaling
        )
        head_onehot = (head_part[:, None] == group_ids[None, :]).astype(jnp.float32)
        grad_k = grad_k + jnp.einsum("ng,nkd->gkd", head_onehot, part_dk, precision=highest)
        grad_v = grad_v + jnp.einsum("ng,nkd->gkd", head_onehot, part_dv, precision=highest)
        served_dq = lax.dynamic_update_slice_in_dim(served_dq, part_dq, offset, 0)
        return (grad_k, grad_v, served_dq)

    zeros_heads = jnp.zeros((groups, row_count, head_dim), jnp.float32)
    start_bwd = (zeros_heads, zeros_heads, jnp.zeros((devices, head_dim, tile_rows), jnp.float32))
    rem_dk, rem_dv, served_dq = lax.fori_loop(0, rounds, backward_turn, start_bwd)
    back_dq = lax.all_to_all(
        jnp.take(served_dq, inverse, axis=0).astype(jnp.bfloat16),
        "ctx",
        split_axis=0,
        concat_axis=0,
        tiled=True,
    ).astype(jnp.float32)
    task_dq = jnp.take(back_dq, lookup, axis=0).reshape(
        tiles_dev, groups, others, head_dim, tile_rows
    )
    rem_dq = jnp.sum(jnp.where(active[..., None, None], task_dq, 0.0), axis=2)
    own_dq_t = own_dq.reshape(groups, tiles_dev, tile_rows, head_dim).transpose(1, 0, 2, 3)
    total_dq = own_dq_t + rem_dq.transpose(0, 1, 3, 2)
    grad_query = total_dq.transpose(0, 2, 1, 3).reshape(row_count, columns).astype(jnp.bfloat16)
    grad_key = (own_dk + rem_dk).transpose(1, 0, 2).reshape(row_count, columns).astype(jnp.bfloat16)
    grad_value = (
        (own_dv + rem_dv).transpose(1, 0, 2).reshape(row_count, columns).astype(jnp.bfloat16)
    )
    return (attn_out, grad_query, grad_key, grad_value)


def solution(mesh):
    placed = (
        P("ctx", "head"),
        P("ctx", "head"),
        P("ctx", "head"),
        P("ctx", "head"),
        P("ctx", "head", None),
    )
    return jax.shard_map(
        local,
        mesh=mesh,
        in_specs=placed,
        out_specs=(P("ctx", "head"), P("ctx", "head"), P("ctx", "head"), P("ctx", "head")),
        check_vma=False,
    )
```

profile of v0, /device:TPU:1, one launch (start us, length us, event | category | flops | bytes accessed | tf_op | source)
XLA Modules:
  0.0 1118.9 jit_solution(2755276544364780009)
XLA Ops:
  5.0 2.7 copy.197
  7.7 20.5 %all-to-all-start = ((bf16[128,64,128]{2,1,0:T(8,128)(2,1)}), bf16[128,64,128]{2,1,0:T(8,128)(2,1)S(1)}, u32[]{:S(2)}, u32[]{:S(2)}) async-start(bf16[128,64,128]{2,1,0:T(8,128)(2,1)} %copy.197), calls=%async_computation | async-start | bytes 4194304 | tf_op jit(solution)/shard_map/all_to_all | solution.py:77
  29.1 186.2 %all_gather.3 = s32[512,4,4]{2,1,0:T(4,128)S(1)} all-gather(s32[4,4,4]{2,1,0:T(4,128)S(1)} %copy-done.13), channel_id=1, replica_groups=mesh['ctx'=128,'head'=4] {'ctx'}, dimensions={0}, use_global_device_ids=true | all-gather | bytes 33024 | tf_op jit(solution)/shard_map/all_gather | solution.py:55
  215.3 3.3 select_reduce_fusion.1
  218.6 3.4 reduce_or.9
  223.3 2.5 sort.31
  225.8 2.5 sort.32
  228.4 2.0 copy.190
  236.4 1.9 copy.203
  238.3 2.0 reshape.321
  241.2 25.5 %while.58 = (s32[]{:T(128)}, f32[4,512,64]{1,2,0:T(8,128)}, f32[4,512]{1,0:T(4,128)S(1)}, bf16[4,512,64]{2,1,0:T(8,128)(2,1)}, bf16[4,512,64]{2,1,0:T(8,128)(2,1...) while((s32[]{:T(128)}, f32[4,512,64]{1,2,0:T(8,128)}, ...), condition=%wide.region_9.10_spmd.clone, body=%wide.region_0.9_spmd.clone.sunk | while | flops 43353092 | bytes 3179745 | solution.py:100
  266.7 2.1 gather_fusion.5
  268.8 3.2 broadcast_select_fusion.4
  272.0 2.5 broadcast.207
  274.4 80.6 %while.57 = (s32[]{:T(128)}, f32[128,64,128]{2,1,0:T(8,128)}, f32[128,128]{1,0:T(8,128)S(1)}, s32[]{:T(128)}, s32[128]{0:T(128)S(1)}, /*index=5*/bf16[4,512,64]{...) while((s32[]{:T(128)}, f32[128,64,128]{2,1,0:T(8,128)}, ...), condition=%wide.region_18.20_spmd, body=%wide.region_15.19_spmd.sunk | while | flops 138936384 | bytes 12489103 | solution.py:126
  276.2 1.9 multiply_reduce_fusion.4
  284.2 1.9 multiply_reduce_fusion.4
  292.3 1.9 multiply_reduce_fusion.4
  300.3 1.9 multiply_reduce_fusion.4
  308.4 1.9 multiply_reduce_fusion.4
  316.5 1.9 multiply_reduce_fusion.4
  324.5 1.9 multiply_reduce_fusion.4
  332.6 1.9 multiply_reduce_fusion.4
  340.7 1.9 multiply_reduce_fusion.4
  348.8 1.9 multiply_reduce_fusion.4
  356.4 53.7 %all-to-all-start.1 = ((f32[128,1,128]{2,1,0:T(1,128)}), f32[128,1,128]{2,1,0:T(1,128)S(1)}, u32[]{:S(2)}, u32[]{:S(2)}) async-start(f32[128,1,128]{2,1,0:T(1,128)} %bitcast.19), calls=%async_computation.1 | async-start | bytes 131072 | tf_op jit(solution)/shard_map/all_to_all | solution.py:131
  410.2 15.1 %all-to-all-done.1 = f32[128,1,128]{2,1,0:T(1,128)S(1)} async-done(((f32[128,1,128]{2,1,0:T(1,128)}), f32[128,1,128]{2,1,0:T(1,128)S(1)}, u32[]{:S(2)}, u32[]{:S(2)}) %all-to-all-start.1) | async-done | bytes 65568 | tf_op jit(solution)/shard_map/all_to_all | solution.py:131
  426.3 2.2 convolution_bitcast_fusion
  428.4 2.9 copy.215
  431.4 6.6 all-to-all-start.3
  438.0 5.0 gather_fusion.8
  442.9 4.5 broadcast_select_fusion.3
  447.4 89.8 %all-to-all-done.3 = bf16[128,64,128]{2,1,0:T(8,128)(2,1)S(1)} async-done(((bf16[128,64,128]{2,1,0:T(8,128)(2,1)}), bf16[128,64,128]{2,1,0:T(8,128)(2,1)S(1)}, u32[]{:S(2)}, u32[]{:S(2)}) %all-to-all-start.3) | async-done | bytes 2097184 | tf_op jit(solution)/shard_map/all_to_all | solution.py:207
  537.2 9.2 all-to-all-start.2
  546.5 2.0 reshape.313
  548.5 1.9 broadcast_convert_fusion
  550.6 2.2 gather_fusion.10
  552.8 3.4 select_convert_fusion.1
  556.2 175.4 %all-to-all-done.2 = f32[128,64,128]{2,1,0:T(8,128)} async-done(((f32[128,64,128]{2,1,0:T(8,128)}), f32[128,64,128]{2,1,0:T(8,128)}, u32[]{:S(2)}, u32[]{:S(2)}) %all-to-all-start.2) | async-done | bytes 4194336 | tf_op jit(solution)/shard_map/all_to_all | solution.py:128
  731.7 2.8 gather_fusion.9
  737.6 12.1 %all-to-all-start.4 = ((f32[128,1,128]{2,1,0:T(1,128)}), f32[128,1,128]{2,1,0:T(1,128)S(1)}, u32[]{:S(2)}, u32[]{:S(2)}) async-start(f32[128,1,128]{2,1,0:T(1,128)} %bitcast.48), calls=%async_computation.4 | async-start | bytes 131072 | tf_op jit(solution)/shard_map/all_to_all | solution.py:208
  750.9 13.8 %all-to-all-done.4 = f32[128,1,128]{2,1,0:T(1,128)S(1)} async-done(((f32[128,1,128]{2,1,0:T(1,128)}), f32[128,1,128]{2,1,0:T(1,128)S(1)}, u32[]{:S(2)}, u32[]{:S(2)}) %all-to-all-start.4) | async-done | bytes 65568 | tf_op jit(solution)/shard_map/all_to_all | solution.py:208
  767.2 146.0 %while.60 = (s32[]{:T(128)}, f32[4,512,64]{1,0,2:T(4,128)}, f32[4,512,64]{1,0,2:T(4,128)}, bf16[128,64,128]{2,1,0:T(8,128)(2,1)}, s32[]{:T(128)}, /*index=5*/s32...) while((s32[]{:T(128)}, f32[4,512,64]{1,0,2:T(4,128)}, ...), condition=%wide.region_26.31_spmd.clone, body=%wide.region_25.30_spmd.clone.sunk | while | flops 366281888 | bytes 31752884 | solution.py:232
  772.5 2.1 multiply_convert_fusion.4
  787.1 2.1 multiply_convert_fusion.4
  798.1 1.8 fusion.316
  801.6 2.1 multiply_convert_fusion.4
  816.2 2.1 multiply_convert_fusion.4
  830.8 2.1 multiply_convert_fusion.4
  845.4 2.1 multiply_convert_fusion.4
  860.0 2.1 multiply_convert_fusion.4
  871.0 1.8 fusion.316
  874.5 2.1 multiply_convert_fusion.4
  889.1 2.1 multiply_convert_fusion.4
  900.2 1.8 fusion.316
  903.7 2.1 multiply_convert_fusion.4
  913.2 2.5 gather_fusion.12
  915.8 1.8 select_convert_fusion
  917.6 94.1 %all-to-all-start.5 = ((bf16[128,64,128]{2,1,0:T(8,128)(2,1)}), bf16[128,64,128]{2,1,0:T(8,128)(2,1)S(1)}, u32[]{:S(2)}, u32[]{:S(2)}) async-start(bf16[128,64,128]{2,1,0:T(8,128)(2,1)} %select_convert_fusion), calls=%async_computation.5 | async-start | bytes 4194304 | tf_op jit(solution)/shard_map/all_to_all | solution.py:233
  1014.3 73.1 %while.59 = (s32[]{:T(128)}, f32[4,512,64]{1,2,0:T(8,128)}, f32[4,512,64]{1,2,0:T(8,128)}, f32[4,512,64]{1,2,0:T(8,128)}, bf16[4,512,64]{2,1,0:T(8,128)(2,1)}, /...) while((s32[]{:T(128)}, f32[4,512,64]{1,2,0:T(8,128)}, ...), condition=%wide.region_24.29_spmd.clone, body=%wide.region_23.28_spmd.clone.sunk | while | flops 106577920 | bytes 5930805 | solution.py:195
  1090.0 2.2 fusion.157
  1094.9 16.0 %all-to-all-done.5 = bf16[128,64,128]{2,1,0:T(8,128)(2,1)S(1)} async-done(((bf16[128,64,128]{2,1,0:T(8,128)(2,1)}), bf16[128,64,128]{2,1,0:T(8,128)(2,1)S(1)}, u32[]{:S(2)}, u32[]{:S(2)}) %all-to-all-start.5) | async-done | bytes 2097184 | tf_op jit(solution)/shard_map/all_to_all | solution.py:233
  1110.9 2.4 convert_element_type.185
  1113.3 2.8 gather_fusion.13
  (567 shorter events, 310.1 us)
Async XLA Ops:
  7.7 20.6 %copy-start.12 = (bf16[512,256]{1,0:T(8,128)(2,1)S(1)}, bf16[512,256]{1,0:T(8,128)(2,1)}, u32[]{:S(2)}) copy-start(bf16[512,256]{1,0:T(8,128)(2,1)} %param.21) | copy-start | bytes 786436
  7.7 21.4 %copy-start.13 = (s32[4,4,4]{2,1,0:T(4,128)S(1)}, s32[4,4,4]{2,1,0:T(4,128)}, u32[]{:S(2)}) copy-start(s32[4,4,4]{2,1,0:T(4,128)} %param.25) | copy-start | bytes 772
  7.7 259.0 %all-to-all-start = ((bf16[128,64,128]{2,1,0:T(8,128)(2,1)}), bf16[128,64,128]{2,1,0:T(8,128)(2,1)S(1)}, u32[]{:S(2)}, u32[]{:S(2)}) async-start(bf16[128,64,128]{2,1,0:T(8,128)(2,1)} %copy.197), calls=%async_computation | async-start | bytes 4194304 | tf_op jit(solution)/shard_map/all_to_all | solution.py:77
  29.1 202.6 %copy-start.14 = (s32[512]{0:T(512)}, s32[512]{0:T(512)S(1)}, u32[]{:S(2)}) copy-start(s32[512]{0:T(512)S(1)} %iota.43) | copy-start | bytes 6148
  233.5 7.7 slice-start
  279.8 1.2 copy-start.1
  287.8 1.2 copy-start.1
  356.4 68.8 %all-to-all-start.1 = ((f32[128,1,128]{2,1,0:T(1,128)}), f32[128,1,128]{2,1,0:T(1,128)S(1)}, u32[]{:S(2)}, u32[]{:S(2)}) async-start(f32[128,1,128]{2,1,0:T(1,128)} %bitcast.19), calls=%async_computation.1 | async-start | bytes 131072 | tf_op jit(solution)/shard_map/all_to_all | solution.py:131
  431.4 105.8 %all-to-all-start.3 = ((bf16[128,64,128]{2,1,0:T(8,128)(2,1)}), bf16[128,64,128]{2,1,0:T(8,128)(2,1)S(1)}, u32[]{:S(2)}, u32[]{:S(2)}) async-start(bf16[128,64,128]{2,1,0:T(8,128)(2,1)} %copy.215), calls=%async_computation.3 | async-start | bytes 4194304 | tf_op jit(solution)/shard_map/all_to_all | solution.py:207
  537.2 194.5 %all-to-all-start.2 = ((f32[128,64,128]{2,1,0:T(8,128)}), f32[128,64,128]{2,1,0:T(8,128)}, u32[]{:S(2)}, u32[]{:S(2)}) async-start(f32[128,64,128]{2,1,0:T(8,128)} %broadcast_select_fusion.3), calls=%async_computation.2 | async-start | bytes 8388608 | tf_op jit(solution)/shard_map/all_to_all | solution.py:128
  737.6 27.1 %all-to-all-start.4 = ((f32[128,1,128]{2,1,0:T(1,128)}), f32[128,1,128]{2,1,0:T(1,128)S(1)}, u32[]{:S(2)}, u32[]{:S(2)}) async-start(f32[128,1,128]{2,1,0:T(1,128)} %bitcast.48), calls=%async_computation.4 | async-start | bytes 131072 | tf_op jit(solution)/shard_map/all_to_all | solution.py:208
  774.6 1.3 copy-start.2
  777.3 3.2 copy-start.3
  777.3 1.7 copy-start.5
  777.3 3.2 copy-start
  780.5 1.3 copy-start.6
  789.2 1.3 copy-start.2
  791.9 3.2 copy-start.3
  791.9 1.7 copy-start.5
  791.9 3.2 copy-start
  795.1 1.3 copy-start.6
  803.7 1.3 copy-start.2
  806.4 3.2 copy-start.3
  806.4 1.7 copy-start.5
  806.5 3.2 copy-start
  809.6 1.3 copy-start.6
  818.3 1.3 copy-start.2
  821.0 3.2 copy-start.3
  821.0 1.7 copy-start.5
  821.0 3.2 copy-start
  824.2 1.3 copy-start.6
  832.9 1.3 copy-start.2
  835.6 3.2 copy-start.3
  835.6 1.7 copy-start.5
  835.6 3.2 copy-start
  838.8 1.3 copy-start.6
  847.5 1.3 copy-start.2
  850.2 3.2 copy-start.3
  850.2 1.7 copy-start.5
  850.2 3.2 copy-start
  853.4 1.3 copy-start.6
  862.0 1.3 copy-start.2
  864.8 3.2 copy-start.3
  864.8 1.7 copy-start.5
  864.8 3.2 copy-start
  867.9 1.3 copy-start.6
  876.6 1.3 copy-start.2
  879.3 3.2 copy-start.3
  879.3 1.7 copy-start.5
  879.4 3.2 copy-start
  882.5 1.3 copy-start.6
  891.2 1.3 copy-start.2
  893.9 3.2 copy-start.3
  893.9 1.7 copy-start.5
  893.9 3.2 copy-start
  897.1 1.3 copy-start.6
  905.8 1.3 copy-start.2
  908.5 3.2 copy-start.3
  908.5 1.7 copy-start.5
  908.5 3.2 copy-start
  911.7 1.3 copy-start.6
  917.6 193.3 %all-to-all-start.5 = ((bf16[128,64,128]{2,1,0:T(8,128)(2,1)}), bf16[128,64,128]{2,1,0:T(8,128)(2,1)S(1)}, u32[]{:S(2)}, u32[]{:S(2)}) async-start(bf16[128,64,128]{2,1,0:T(8,128)(2,1)} %select_convert_fusion), calls=%async_computation.5 | async-start | bytes 4194304 | tf_op jit(solution)/shard_map/all_to_all | solution.py:233
  1087.4 2.6 copy-start.4
  1087.4 2.6 copy-start.7
  (12 other events, 13.9 us)
where the time goes:
time: 1130 us; the launch traced here: 1120 us
  waiting for transfers between devices  310 us (27%)
  matrix products  238 us (21%)
  starting transfers between devices  196 us (17%)
  blocking collectives  186 us (16%)
  local copies, waits for them, and re-layouts  132 us (12%)
  other arithmetic  52.7 us (5%)
    all_gather x1, blocking collectives, local(): all_picks = lax.all_gather(picks, 'ctx', axis=0, tiled=True)  186 us
    all_to_all x1, waiting for transfers between devices, local(): lax.all_to_all(jnp.take(served_out, inverse, axis=0), 'ctx', split_axis=0...  175 us
    all_to_all x1, starting transfers between devices, local(): lax.all_to_all(jnp.take(served_dq, inverse, axis=0).astype(jnp.bfloat16),...  94.1 us
    all_to_all x1, waiting for transfers between devices, local(): lax.all_to_all(send_g, 'ctx', split_axis=0, concat_axis=0, tiled=True)  89.8 us
    all_to_all x1, starting transfers between devices, local(): lax.all_to_all(jnp.take(served_lse, inverse, axis=0), 'ctx', split_axis=0...  53.7 us
  transfers between devices with their start and end apart: 6, of which 5 were waited for; matrix products, arithmetic and copies ran while one was open for 14% of the time, Pallas kernels for 0%

commit v1 on v0

v1 whole, which is shorter than its diff:
```python
import functools

import jax
import jax.numpy as jnp
from jax import lax
from jax.experimental import pallas as pl
from jax.experimental.pallas import tpu as pltpu
from jax.sharding import PartitionSpec as P

MESH = pl.DeviceIdType.MESH
f32, bf16 = jnp.float32, jnp.bfloat16
HEADS, TILES, DIM, ROWS = 4, 4, 64, 128
TASKS = HEADS * TILES
OTHERS = 3
KEYS = TILES * ROWS
COLS = HEADS * DIM
PAIR = 2 * ROWS
MSG = 2 * DIM + 16
RET = DIM + 16
FAR = -1e30


def dot(a, b):
    return lax.dot_general(a, b, (((1,), (0,)), ((), ())), preferred_element_type=f32)


def dot_rows(a, b):
    return lax.dot_general(a, b, (((1,), (1,)), ((), ())), preferred_element_type=f32)


def kernel(
    n, table, q_ref, k_ref, v_ref, g_ref, ao_ref, dq_ref, dk_ref, dv_ref,
    qg, k8, k8t, vt, kept, inv_sum, sent, got, back, ret, w_sent, w_got, dq_sent, dq_got,
    own_out, own_lse, own_w, w_all, attn, own_dq, dk_acc, dv_acc,
    send_a, send_b, recv_a, recv_b,
):
    me = lax.axis_index("ctx")
    first = (me + 1) // 2
    last = n // 2

    def remote(src, dst, send, recv, peer):
        return pltpu.make_async_remote_copy(
            src_ref=src, dst_ref=dst, send_sem=send.at[peer], recv_sem=recv.at[peer],
            device_id={"ctx": peer}, device_id_type=MESH,
        )

    def push(src, dst, send, recv, peer):
        pltpu.make_async_remote_copy(
            src_ref=src.at[peer], dst_ref=dst.at[me], send_sem=send.at[peer], recv_sem=recv.at[me],
            device_id={"ctx": peer}, device_id_type=MESH,
        ).start()

    barrier = pltpu.get_barrier_semaphore()

    def greet(i, c):
        @pl.when(i != me)
        def _():
            pl.semaphore_signal(barrier, inc=1, device_id={"ctx": i}, device_id_type=MESH)

        return c

    lax.fori_loop(0, n, greet, 0)

    for t in range(TILES):
        rows = slice(t * ROWS, (t + 1) * ROWS)
        q_t = q_ref[rows, :].astype(f32).T.astype(bf16)
        g_t = g_ref[rows, :].astype(f32).T.astype(bf16)
        for h in range(HEADS):
            part = slice(h * DIM, (h + 1) * DIM)
            qg[t * HEADS + h, 0:DIM, :] = q_t[part]
            qg[t * HEADS + h, DIM : 2 * DIM, :] = g_t[part]
        k_rows = k_ref[rows, :].astype(f32) * 0.125
        k8[rows, :] = k_rows.astype(bf16)
        k8t[:, rows] = k_rows.T.astype(bf16)
        vt[:, rows] = v_ref[rows, :].astype(f32).T.astype(bf16)
    got[me, :, :] = jnp.zeros((MSG, ROWS), bf16)
    w_got[me, :, :] = jnp.zeros((2, ROWS), f32)

    pl.semaphore_wait(barrier, n - 1)

    lines = lax.broadcasted_iota(jnp.int32, (16, ROWS), 0)

    def send_tile(j, c):
        d = me - 1 - j
        sent[d, 0 : 2 * DIM, :] = qg[table[0, d]]
        sent[d, 2 * DIM : MSG, :] = jnp.where(lines == table[1, d], 1.0, 0.0).astype(bf16)
        push(sent, got, send_a, recv_a, d)
        return c

    lax.fori_loop(0, me, send_tile, 0)

    def spread(x, mask):
        return jnp.concatenate([(x * mask[h : h + 1]).astype(bf16) for h in range(HEADS)], axis=0)

    def choose(x, mask):
        total = x[0:DIM] * mask[0:1]
        for h in range(1, HEADS):
            total += x[h * DIM : (h + 1) * DIM] * mask[h : h + 1]
        return total

    def own_mask(half):
        row = lax.broadcasted_iota(jnp.int32, (16, PAIR), 0)
        lane = lax.broadcasted_iota(jnp.int32, (16, PAIR), 1)
        return jnp.where(row == 2 * half + lane // ROWS, 1.0, 0.0)

    def two(ref, a, b, start, end):
        return jnp.concatenate([ref[a, start:end, :], ref[b, start:end, :]], axis=1)

    def forward(slot, q_exp, mask, causal=None):
        scores = dot(k8[...], q_exp)
        if causal is not None:
            scores = jnp.where(causal, scores, FAR)
        peak = jnp.max(scores, axis=0, keepdims=True)
        e = jnp.exp(scores - peak)
        total = jnp.sum(e, axis=0, keepdims=True)
        e = e.astype(bf16)
        kept[slot] = e
        over = 1.0 / total
        inv_sum[slot] = over
        out = choose(dot(vt[...], e), mask) * over
        return out, peak + jnp.log(total)

    def backward(slot, q_exp, g_t, mask, w, shift):
        over = inv_sum[slot]
        g_exp = spread((g_t.astype(f32) * (w * over)).astype(bf16).astype(f32), mask)
        e = kept[slot]
        grad_prob = dot(v_ref[...], g_exp)
        dscore = (e.astype(f32) * (grad_prob - shift * over)).astype(bf16)
        dk_acc[...] += dot_rows(dscore, q_exp)
        dv_acc[...] += dot_rows(e, g_exp)
        return choose(dot(k8t[...], dscore), mask)

    def own_forward(t, c):
        key = lax.broadcasted_iota(jnp.int32, (KEYS, PAIR), 0)
        query = lax.broadcasted_iota(jnp.int32, (KEYS, PAIR), 1) % ROWS + t * ROWS
        for half in range(2):
            a = t * HEADS + 2 * half
            mask = own_mask(half)
            q_exp = spread(two(qg, a, a + 1, 0, DIM).astype(f32), mask)
            out, lse = forward(last + 2 * t + half, q_exp, mask, key <= query)
            for i in range(2):
                own_out[a + i] = out[:, i * ROWS : (i + 1) * ROWS]
                own_lse[a + i] = lse[:, i * ROWS : (i + 1) * ROWS]
        return c

    lax.fori_loop(0, TILES, own_forward, 0)

    def serve(j, c):
        a, b = 2 * j, 2 * j + 1

        @pl.when(a > me)
        def _():
            remote(sent.at[a], got.at[a], send_a, recv_a, a).wait_recv()

        remote(sent.at[b], got.at[b], send_a, recv_a, b).wait_recv()
        mask = two(got, a, b, 2 * DIM, MSG).astype(f32)
        q_exp = spread(two(got, a, b, 0, DIM).astype(f32), mask)
        out, lse = forward(j, q_exp, mask)
        high = lse.astype(bf16).astype(f32)
        middle = (lse - high).astype(bf16).astype(f32)
        low = lse - high - middle
        row = lax.broadcasted_iota(jnp.int32, (16, PAIR), 0)
        packed = jnp.where(row == 0, high, jnp.where(row == 1, middle, jnp.where(row == 2, low, 0.0))).astype(bf16)
        out = out.astype(bf16)
        back[a, 0:DIM, :] = out[:, :ROWS]
        back[b, 0:DIM, :] = out[:, ROWS:]
        back[a, DIM:RET, :] = packed[:, :ROWS]
        back[b, DIM:RET, :] = packed[:, ROWS:]

        @pl.when(a > me)
        def _():
            push(back, ret, send_a, recv_a, a)

        push(back, ret, send_a, recv_a, b)
        return c

    lax.fori_loop(first, last, serve, 0)

    def wait_return(d, c):
        remote(back.at[d], ret.at[d], send_a, recv_a, d).wait_recv()
        return c

    lax.fori_loop(0, me, wait_return, 0)

    def combine(th, c):
        parts = []
        lse_own = own_lse[th]
        ceiling = lse_own
        for i in range(OTHERS):
            d = table[3, th * OTHERS + i]
            live = jnp.full((1, ROWS), d, jnp.int32) != me
            terms = ret[d, DIM:RET, :].astype(f32)
            lse = jnp.where(live, terms[0:1] + terms[1:2] + terms[2:3], FAR)
            ceiling = jnp.maximum(ceiling, lse)
            parts.append((d, live, lse))
        total = jnp.exp(lse_own - ceiling)
        for _, _, lse in parts:
            total += jnp.exp(lse - ceiling)
        lse_all = ceiling + jnp.log(total)
        w_own = jnp.exp(lse_own - lse_all)
        mixed = w_own * own_out[th]
        weights = []
        for d, live, lse in parts:
            w = jnp.where(live, jnp.exp(lse - lse_all), 0.0)
            mixed += jnp.where(live, w * ret[d, 0:DIM, :].astype(f32), 0.0)
            weights.append(w)
        low = mixed.astype(bf16).astype(f32)
        delta = jnp.sum(qg[th, DIM : 2 * DIM, :].astype(f32) * low, axis=0, keepdims=True)
        attn[th] = low
        own_w[th] = jnp.concatenate([w_own, w_own * delta], axis=0)
        for i, w in enumerate(weights):
            w_all[th * OTHERS + i] = jnp.concatenate([w, w * delta], axis=0)
        return c

    lax.fori_loop(0, TASKS, combine, 0)

    def send_weights(j, c):
        d = me - 1 - j
        w_sent[d] = w_all[table[2, d]]
        push(w_sent, w_got, send_b, recv_b, d)
        return c

    lax.fori_loop(0, me, send_weights, 0)

    for t in range(TILES):
        block = jnp.concatenate([attn[t * HEADS + h] for h in range(HEADS)], axis=0)
        ao_ref[t * ROWS : (t + 1) * ROWS, :] = block.T.astype(bf16)
    dk_acc[...] = jnp.zeros_like(dk_acc)
    dv_acc[...] = jnp.zeros_like(dv_acc)

    def own_backward(t, c):
        for half in range(2):
            a = t * HEADS + 2 * half
            mask = own_mask(half)
            q_exp = spread(two(qg, a, a + 1, 0, DIM).astype(f32), mask)
            rows = jnp.concatenate([own_w[a], own_w[a + 1]], axis=1)
            grad = backward(
                last + 2 * t + half, q_exp, two(qg, a, a + 1, DIM, 2 * DIM), mask, rows[0:1], rows[1:2]
            )
            for i in range(2):
                own_dq[a + i] = grad[:, i * ROWS : (i + 1) * ROWS]
        return c

    lax.fori_loop(0, TILES, own_backward, 0)

    def serve_back(j, c):
        a, b = 2 * j, 2 * j + 1

        @pl.when(a > me)
        def _():
            remote(w_sent.at[a], w_got.at[a], send_b, recv_b, a).wait_recv()

        remote(w_sent.at[b], w_got.at[b], send_b, recv_b, b).wait_recv()
        mask = two(got, a, b, 2 * DIM, MSG).astype(f32)
        q_exp = spread(two(got, a, b, 0, DIM).astype(f32), mask)
        rows = jnp.concatenate([w_got[a], w_got[b]], axis=1)
        grad = backward(j, q_exp, two(got, a, b, DIM, 2 * DIM), mask, rows[0:1], rows[1:2]).astype(bf16)
        dq_sent[a] = grad[:, :ROWS]
        dq_sent[b] = grad[:, ROWS:]

        @pl.when(a > me)
        def _():
            push(dq_sent, dq_got, send_b, recv_b, a)

        push(dq_sent, dq_got, send_b, recv_b, b)
        return c

    lax.fori_loop(first, last, serve_back, 0)
    dk_ref[...] = (dk_acc[...] * 0.125).astype(bf16)
    dv_ref[...] = dv_acc[...].astype(bf16)

    def wait_down(d, c):
        remote(dq_sent.at[d], dq_got.at[d], send_b, recv_b, d).wait_recv()
        return c

    lax.fori_loop(0, me, wait_down, 0)

    def sum_queries(th, c):
        total = own_dq[th]
        for i in range(OTHERS):
            d = table[3, th * OTHERS + i]
            live = jnp.full((1, ROWS), d, jnp.int32) != me
            total += jnp.where(live, dq_got[d].astype(f32), 0.0)
        own_dq[th] = total
        return c

    lax.fori_loop(0, TASKS, sum_queries, 0)
    for t in range(TILES):
        block = jnp.concatenate([own_dq[t * HEADS + h] for h in range(HEADS)], axis=0)
        dq_ref[t * ROWS : (t + 1) * ROWS, :] = block.T.astype(bf16)

    def drain_low(d, c):
        remote(sent.at[d], got.at[d], send_a, recv_a, d).wait_send()
        remote(w_sent.at[d], w_got.at[d], send_b, recv_b, d).wait_send()
        return c

    def drain_high(s, c):
        remote(back.at[s], ret.at[s], send_a, recv_a, s).wait_send()
        remote(dq_sent.at[s], dq_got.at[s], send_b, recv_b, s).wait_send()
        return c

    lax.fori_loop(0, me, drain_low, 0)
    lax.fori_loop(me + 1, n, drain_high, 0)


def local(query, key, value, grad_out, picks):
    n = lax.axis_size("ctx")
    me = lax.axis_index("ctx")
    targets = picks[:, :, 1:].reshape(TASKS * OTHERS)
    peers = jnp.arange(n, dtype=jnp.int32)
    named = (targets[None, :] == peers[:, None]) & (targets != me)[None, :]
    task = jnp.max(jnp.where(named, jnp.arange(TASKS * OTHERS, dtype=jnp.int32)[None, :], -1), axis=1)
    some = jnp.maximum(task, 0)
    tile_head = some // OTHERS
    width = max(n, TASKS * OTHERS)
    rows = [tile_head, jnp.where(task >= 0, tile_head % HEADS, -1), some, targets]
    table = jnp.stack([jnp.pad(r, (0, width - r.shape[0])) for r in rows])
    shape = jax.ShapeDtypeStruct((KEYS, COLS), bf16)
    vmem = pl.BlockSpec(memory_space=pltpu.VMEM)
    return pl.pallas_call(
        functools.partial(kernel, n),
        out_shape=[shape] * 4,
        in_specs=[pl.BlockSpec(memory_space=pltpu.SMEM)] + [vmem] * 4,
        out_specs=[vmem] * 4,
        scratch_shapes=[
            pltpu.VMEM((TASKS, 2 * DIM, ROWS), bf16),
            pltpu.VMEM((KEYS, COLS), bf16),
            pltpu.VMEM((COLS, KEYS), bf16),
            pltpu.VMEM((COLS, KEYS), bf16),
            pltpu.VMEM((n // 2 + TASKS // 2, KEYS, PAIR), bf16),
            pltpu.VMEM((n // 2 + TASKS // 2, 1, PAIR), f32),
            pltpu.VMEM((n, MSG, ROWS), bf16),
            pltpu.VMEM((n, MSG, ROWS), bf16),
            pltpu.VMEM((n, RET, ROWS), bf16),
            pltpu.VMEM((n, RET, ROWS), bf16),
            pltpu.VMEM((n, 2, ROWS), f32),
            pltpu.VMEM((n, 2, ROWS), f32),
            pltpu.VMEM((n, DIM, ROWS), bf16),
            pltpu.VMEM((n, DIM, ROWS), bf16),
            pltpu.VMEM((TASKS, DIM, ROWS), f32),
            pltpu.VMEM((TASKS, 1, ROWS), f32),
            pltpu.VMEM((TASKS, 2, ROWS), f32),
            pltpu.VMEM((TASKS * OTHERS, 2, ROWS), f32),
            pltpu.VMEM((TASKS, DIM, ROWS), f32),
            pltpu.VMEM((TASKS, DIM, ROWS), f32),
            pltpu.VMEM((KEYS, COLS), f32),
            pltpu.VMEM((KEYS, COLS), f32),
            pltpu.SemaphoreType.DMA((n,)),
            pltpu.SemaphoreType.DMA((n,)),
            pltpu.SemaphoreType.DMA((n,)),
            pltpu.SemaphoreType.DMA((n,)),
        ],
        compiler_params=pltpu.CompilerParams(
            collective_id=0, has_side_effects=True, vmem_limit_bytes=56 * 1024 * 1024
        ),
        name="block_sparse",
    )(table, query, key, value, grad_out)


def solution(mesh):
    whole = P("ctx", "head")
    return jax.shard_map(
        local,
        mesh=mesh,
        in_specs=(whole, whole, whole, whole, P("ctx", "head", None)),
        out_specs=(whole, whole, whole, whole),
        check_vma=False,
    )
```

time: 1130 us -> 354 us (0.31)
  Pallas kernels: 0 us -> 347 us
  waiting for transfers between devices: 310 us -> 0 us
  matrix products: 238 us -> 0 us
  starting transfers between devices: 196 us -> 0 us
  blocking collectives: 186 us -> 0 us
  local copies, waits for them, and re-layouts: 132 us -> 5.37 us
  other arithmetic: 52.7 us -> 0.72 us
    pallas_call x0 -> x1, Pallas kernels: none -> 347 us  [local(): pl.pallas_call(functools.partial(kernel, n), out_shape=[shape] * 4, in_sp...]
    all_to_all x6 -> x0, waiting for transfers between devices: 310 us -> none  [the longest x1 175 us: local(): lax.all_to_all(jnp.take(served_out, inverse, axis=0), 'ctx', split_axis=0...]
    dot_general x205 -> x0, matrix products: 238 us -> none  [the longest x10 20.9 us: slot_grads(): jnp.einsum('ndq,nkd->nqk', g_slots, value_rows, preferred_element_type=jn...]
    all_to_all x6 -> x0, starting transfers between devices: 196 us -> none  [the longest x1 94.1 us: local(): lax.all_to_all(jnp.take(served_dq, inverse, axis=0).astype(jnp.bfloat16),...]
    all_gather x1 -> x0, blocking collectives: 186 us -> none  [local(): all_picks = lax.all_gather(picks, 'ctx', axis=0, tiled=True)]
    gather x51 -> x0, local copies, waits for them, and re-layouts: 87.7 us -> none  [the longest x10 17.1 us: slot_grads(): value_rows = jnp.take(v_heads, head_ids, axis=0)]
    reduce_sum x31 -> x0, other arithmetic: 12.2 us -> none  [the longest x10 5.46 us: attend_slots(): jnp.sum(jnp.exp(scores - peak_score), axis=-1, keepdims=True)]
    convert_element_type x7 -> x0, other arithmetic: 11.8 us -> none  [the longest x1 3.44 us: local(): g_sorted = jnp.take(recv_g, ranking, axis=0).astype(jnp.bfloat16)]
  transfers between devices with their start and end apart: 6 -> 0, of which waited for: 5 -> 0; matrix products, arithmetic and copies ran while one was open for 14% -> 0% of each run, Pallas kernels for 0% -> 0%
where the time goes in v1:
time: 354 us
  Pallas kernels  347 us (98%)
  local copies, waits for them, and re-layouts  5.37 us (2%)
    pallas_call x1, Pallas kernels, local(): pl.pallas_call(functools.partial(kernel, n), out_shape=[shape] * 4, in_sp...  347 us

profile of v1, /device:TPU:1, one launch (start us, length us, event | category | flops | bytes accessed | tf_op | source)
XLA Modules:
  0.0 353.5 jit_solution(659953890105912836)
XLA Ops:
  0.6 0.8 slice.3
  1.4 0.1 eq.17
  1.5 0.1 select_reduce_fusion
  1.7 0.6 pad_add_fusion.table
  2.2 346.8 %block_sparse.1 = (bf16[512,256]{1,0:T(8,128)(2,1)}, bf16[512,256]{1,0:T(8,128)(2,1)}, bf16[512,256]{1,0:T(8,128)(2,1)}, bf16[512,256]{1,0:T(8,128)(2,1)}) custom-call(s32[4,128]{1,0:T(4,128)} %pad_add_fusion.table, bf16[512,256]{1,0:T(8,128)(2,1)} %q_ref.1, bf16[512,256]{1,0:T(8,128)(2,1)} %k_ref.1, bf16[512,256]{1,0:T(8,128)(2,1)} %v_ref.1, ...), custom_call_target="tpu_custom_call" | custom-call | tf_op jit(solution)/shard_map/block_sparse/pallas_call | solution.py:320
  349.0 0.0 copy-start.2
  349.0 1.7 copy.13
  350.8 0.0 copy-done.2
  350.8 0.0 copy-start.1
  350.8 0.7 copy.14
  351.5 0.3 copy-done.1
  351.8 0.0 copy-start
  351.8 0.7 copy.15
  352.5 0.3 copy-done
  352.8 0.7 copy.16
  (3 shorter events, 0.0 us)
Async XLA Ops:
  349.0 1.7 copy-start.2
  350.8 1.0 copy-start.1
  351.8 1.0 copy-start

commit v2 on v1

v2 whole, which is shorter than its diff:
```python
import functools

import jax
import jax.numpy as jnp
from jax import lax
from jax.experimental import pallas as pl
from jax.experimental.pallas import tpu as pltpu
from jax.sharding import PartitionSpec as P

MESH = pl.DeviceIdType.MESH
f32, bf16 = jnp.float32, jnp.bfloat16
HEADS, TILES, DIM, ROWS = 4, 4, 64, 128
TASKS = HEADS * TILES
OTHERS = 3
KEYS = TILES * ROWS
COLS = HEADS * DIM
PAIR = 2 * ROWS
FAR = -1e30


def dot(a, b):
    return lax.dot_general(a, b, (((1,), (0,)), ((), ())), preferred_element_type=f32)


def dot_rows(a, b):
    return lax.dot_general(a, b, (((1,), (1,)), ((), ())), preferred_element_type=f32)


def kernel(
    n, table, q_ref, k_ref, v_ref, g_ref, ao_ref, dq_ref, dk_ref, dv_ref,
    q_t, g_t, k8, k8t, vt, kept, sent, got, code_sent, code_got, back, ret, lse_sent, lse_got,
    g_all, g_sent, g_got, c_all, c_sent, c_got, dq_sent, dq_got,
    own_out, own_lse, own_g, own_c, attn, own_dq, dk_acc, dv_acc,
    send_a, send_b, send_c, send_d, recv_a, recv_b, recv_c, recv_d,
):
    me = lax.axis_index("ctx")
    first = (me + 1) // 2
    last = n // 2
    quarter = n // 4
    depth = quarter // 2
    my_x, my_z, my_core = me // quarter, (me // 2) % depth, me % 2

    def along(i):
        return jnp.where(i % 2 == 0, i // 2, depth - (i + 1) // 2)

    def peer_of(i):
        x = (my_x + 1 + i // quarter) % 4
        z = (my_z + along((i // 2) % depth)) % depth
        return x * quarter + z * 2 + (my_core + i) % 2

    def source_pair(m):
        x = (my_x + 3 - m % 4) % 4
        return x * depth + (my_z + depth - along(m // 4)) % depth

    def remote(src, dst, send, recv, peer):
        return pltpu.make_async_remote_copy(
            src_ref=src, dst_ref=dst, send_sem=send.at[peer], recv_sem=recv.at[peer],
            device_id={"ctx": peer}, device_id_type=MESH,
        )

    def push(src, dst, send, recv, peer):
        pltpu.make_async_remote_copy(
            src_ref=src.at[peer], dst_ref=dst.at[me], send_sem=send.at[peer], recv_sem=recv.at[me],
            device_id={"ctx": peer}, device_id_type=MESH,
        ).start()

    barrier = pltpu.get_barrier_semaphore()

    def greet(i, c):
        @pl.when(i != me)
        def _():
            pl.semaphore_signal(barrier, inc=1, device_id={"ctx": i}, device_id_type=MESH)

        return c

    lax.fori_loop(0, n, greet, 0)

    for t in range(TILES):
        rows = slice(t * ROWS, (t + 1) * ROWS)
        q_rows = q_ref[rows, :].astype(f32).T.astype(bf16)
        g_rows = g_ref[rows, :].astype(f32).T.astype(bf16)
        for h in range(HEADS):
            part = slice(h * DIM, (h + 1) * DIM)
            q_t[t * HEADS + h] = q_rows[part]
            g_t[t * HEADS + h] = g_rows[part]
        k_rows = k_ref[rows, :].astype(f32) * 0.125
        k8[rows, :] = k_rows.astype(bf16)
        k8t[:, rows] = k_rows.T.astype(bf16)
        vt[:, rows] = v_ref[rows, :].astype(f32).T.astype(bf16)
    got[me] = jnp.zeros((DIM, ROWS), bf16)
    code_got[me] = jnp.full((1, ROWS), -1.0, f32)
    g_got[me] = jnp.zeros((DIM, ROWS), bf16)
    c_got[me] = jnp.zeros((1, ROWS), f32)

    pl.semaphore_wait(barrier, n - 1)

    def send_tile(i, c):
        d = peer_of(i)

        @pl.when(d < me)
        def _():
            sent[d] = q_t[table[0, d]]
            code_sent[d] = jnp.full((1, ROWS), table[1, d], jnp.int32).astype(f32)
            push(code_sent, code_got, send_c, recv_c, d)
            push(sent, got, send_a, recv_a, d)

        return c

    lax.fori_loop(0, n, send_tile, 0)

    def spread(x, mask):
        return jnp.concatenate([(x * mask[h : h + 1]).astype(bf16) for h in range(HEADS)], axis=0)

    def choose(x, mask):
        total = x[0:DIM] * mask[0:1]
        for h in range(1, HEADS):
            total += x[h * DIM : (h + 1) * DIM] * mask[h : h + 1]
        return total

    def own_mask(half):
        row = lax.broadcasted_iota(jnp.int32, (8, PAIR), 0)
        lane = lax.broadcasted_iota(jnp.int32, (8, PAIR), 1)
        return jnp.where(row == 2 * half + lane // ROWS, 1.0, 0.0)

    def two(ref, a, b):
        return jnp.concatenate([ref[a], ref[b]], axis=1)

    def forward(slot, q_exp, mask, causal=None):
        scores = dot(k8[...], q_exp)
        if causal is not None:
            scores = jnp.where(causal, scores, FAR)
        peak = jnp.max(scores, axis=0, keepdims=True)
        e = jnp.exp(scores - peak)
        total = jnp.sum(e, axis=0, keepdims=True)
        e = e.astype(bf16)
        kept[slot] = e
        over = 1.0 / total
        out = choose(dot(vt[...], e), mask) * over
        return out, jnp.concatenate([peak + jnp.log(total), over], axis=0)

    def backward(slot, q_exp, g_exp, mask, shift):
        e = kept[slot]
        grad_prob = dot(v_ref[...], g_exp)
        dscore = (e.astype(f32) * (grad_prob - shift)).astype(bf16)
        dk_acc[...] += dot_rows(dscore, q_exp)
        dv_acc[...] += dot_rows(e, g_exp)
        return choose(dot(k8t[...], dscore), mask)

    def own_forward(t, c):
        key = lax.broadcasted_iota(jnp.int32, (KEYS, PAIR), 0)
        query = lax.broadcasted_iota(jnp.int32, (KEYS, PAIR), 1) % ROWS + t * ROWS
        for half in range(2):
            a = t * HEADS + 2 * half
            mask = own_mask(half)
            q_exp = spread(two(q_t, a, a + 1).astype(f32), mask)
            out, lse = forward(last + 2 * t + half, q_exp, mask, key <= query)
            for i in range(2):
                own_out[a + i] = out[:, i * ROWS : (i + 1) * ROWS]
                own_lse[a + i] = lse[:, i * ROWS : (i + 1) * ROWS]
        return c

    lax.fori_loop(0, TILES, own_forward, 0)

    def masks(a, b):
        code = jnp.concatenate([code_got[a], code_got[b]], axis=1)
        row = lax.broadcasted_iota(jnp.int32, (8, PAIR), 0).astype(f32)
        return jnp.where(row == code, 1.0, 0.0)

    def serve(m, c):
        j = source_pair(m)

        @pl.when(j >= first)
        def _():
            serve_pair(j)

        return c

    def serve_pair(j):
        a, b = 2 * j, 2 * j + 1

        @pl.when(a > me)
        def _():
            remote(code_sent.at[a], code_got.at[a], send_c, recv_c, a).wait_recv()
            remote(sent.at[a], got.at[a], send_a, recv_a, a).wait_recv()

        remote(code_sent.at[b], code_got.at[b], send_c, recv_c, b).wait_recv()
        remote(sent.at[b], got.at[b], send_a, recv_a, b).wait_recv()
        mask = masks(a, b)
        q_exp = spread(two(got, a, b).astype(f32), mask)
        out, lse = forward(j, q_exp, mask)
        out = out.astype(bf16)
        for i, s in enumerate((a, b)):
            back[s] = out[:, i * ROWS : (i + 1) * ROWS]
            lse_sent[s] = lse[:, i * ROWS : (i + 1) * ROWS]

        @pl.when(a > me)
        def _():
            push(lse_sent, lse_got, send_c, recv_c, a)
            push(back, ret, send_a, recv_a, a)

        push(lse_sent, lse_got, send_c, recv_c, b)
        push(back, ret, send_a, recv_a, b)

    lax.fori_loop(0, last, serve, 0)

    def wait_return(d, c):
        remote(lse_sent.at[d], lse_got.at[d], send_c, recv_c, d).wait_recv()
        remote(back.at[d], ret.at[d], send_a, recv_a, d).wait_recv()
        return c

    lax.fori_loop(0, me, wait_return, 0)

    def combine(th, c):
        parts = []
        lse_own = own_lse[th, 0:1, :]
        ceiling = lse_own
        for i in range(OTHERS):
            d = table[3, th * OTHERS + i]
            live = jnp.full((1, ROWS), d, jnp.int32) != me
            rows = lse_got[d]
            lse = jnp.where(live, rows[0:1], FAR)
            ceiling = jnp.maximum(ceiling, lse)
            parts.append((d, live, lse, rows[1:2]))
        total = jnp.exp(lse_own - ceiling)
        for _, _, lse, _ in parts:
            total += jnp.exp(lse - ceiling)
        lse_all = ceiling + jnp.log(total)
        w_own = jnp.exp(lse_own - lse_all)
        mixed = w_own * own_out[th]
        weights = []
        for d, live, lse, over in parts:
            w = jnp.where(live, jnp.exp(lse - lse_all), 0.0)
            mixed += jnp.where(live, w * ret[d].astype(f32), 0.0)
            weights.append(jnp.where(live, w * over, 0.0))
        low = mixed.astype(bf16).astype(f32)
        g = g_t[th].astype(f32)
        delta = jnp.sum(g * low, axis=0, keepdims=True)
        attn[th] = low
        w_own = w_own * own_lse[th, 1:2, :]
        own_g[th] = (w_own * g).astype(bf16)
        own_c[th] = w_own * delta
        for i, w in enumerate(weights):
            g_all[th * OTHERS + i] = (w * g).astype(bf16)
            c_all[th * OTHERS + i] = w * delta
        return c

    lax.fori_loop(0, TASKS, combine, 0)

    def send_grad(i, c):
        d = peer_of(i)

        @pl.when(d < me)
        def _():
            c_sent[d] = c_all[table[2, d]]
            g_sent[d] = g_all[table[2, d]]
            push(c_sent, c_got, send_d, recv_d, d)
            push(g_sent, g_got, send_b, recv_b, d)

        return c

    lax.fori_loop(0, n, send_grad, 0)

    for t in range(TILES):
        block = jnp.concatenate([attn[t * HEADS + h] for h in range(HEADS)], axis=0)
        ao_ref[t * ROWS : (t + 1) * ROWS, :] = block.T.astype(bf16)
    dk_acc[...] = jnp.zeros_like(dk_acc)
    dv_acc[...] = jnp.zeros_like(dv_acc)

    def own_backward(t, c):
        for half in range(2):
            a = t * HEADS + 2 * half
            mask = own_mask(half)
            q_exp = spread(two(q_t, a, a + 1).astype(f32), mask)
            g_exp = spread(two(own_g, a, a + 1).astype(f32), mask)
            grad = backward(last + 2 * t + half, q_exp, g_exp, mask, two(own_c, a, a + 1))
            for i in range(2):
                own_dq[a + i] = grad[:, i * ROWS : (i + 1) * ROWS]
        return c

    lax.fori_loop(0, TILES, own_backward, 0)

    def serve_back(m, c):
        j = source_pair(m)

        @pl.when(j >= first)
        def _():
            serve_back_pair(j)

        return c

    def serve_back_pair(j):
        a, b = 2 * j, 2 * j + 1

        @pl.when(a > me)
        def _():
            remote(c_sent.at[a], c_got.at[a], send_d, recv_d, a).wait_recv()
            remote(g_sent.at[a], g_got.at[a], send_b, recv_b, a).wait_recv()

        remote(c_sent.at[b], c_got.at[b], send_d, recv_d, b).wait_recv()
        remote(g_sent.at[b], g_got.at[b], send_b, recv_b, b).wait_recv()
        mask = masks(a, b)
        q_exp = spread(two(got, a, b).astype(f32), mask)
        g_exp = spread(two(g_got, a, b).astype(f32), mask)
        grad = backward(j, q_exp, g_exp, mask, two(c_got, a, b)).astype(bf16)
        for i, s in enumerate((a, b)):
            dq_sent[s] = grad[:, i * ROWS : (i + 1) * ROWS]

        @pl.when(a > me)
        def _():
            push(dq_sent, dq_got, send_b, recv_b, a)

        push(dq_sent, dq_got, send_b, recv_b, b)

    lax.fori_loop(0, last, serve_back, 0)
    dk_ref[...] = (dk_acc[...] * 0.125).astype(bf16)
    dv_ref[...] = dv_acc[...].astype(bf16)

    def wait_down(d, c):
        remote(dq_sent.at[d], dq_got.at[d], send_b, recv_b, d).wait_recv()
        return c

    lax.fori_loop(0, me, wait_down, 0)

    def sum_queries(th, c):
        total = own_dq[th]
        for i in range(OTHERS):
            d = table[3, th * OTHERS + i]
            live = jnp.full((1, ROWS), d, jnp.int32) != me
            total += jnp.where(live, dq_got[d].astype(f32), 0.0)
        own_dq[th] = total
        return c

    lax.fori_loop(0, TASKS, sum_queries, 0)
    for t in range(TILES):
        block = jnp.concatenate([own_dq[t * HEADS + h] for h in range(HEADS)], axis=0)
        dq_ref[t * ROWS : (t + 1) * ROWS, :] = block.T.astype(bf16)

    def drain_low(d, c):
        remote(code_sent.at[d], code_got.at[d], send_c, recv_c, d).wait_send()
        remote(sent.at[d], got.at[d], send_a, recv_a, d).wait_send()
        remote(c_sent.at[d], c_got.at[d], send_d, recv_d, d).wait_send()
        remote(g_sent.at[d], g_got.at[d], send_b, recv_b, d).wait_send()
        return c

    def drain_high(s, c):
        remote(lse_sent.at[s], lse_got.at[s], send_c, recv_c, s).wait_send()
        remote(back.at[s], ret.at[s], send_a, recv_a, s).wait_send()
        remote(dq_sent.at[s], dq_got.at[s], send_b, recv_b, s).wait_send()
        return c

    lax.fori_loop(0, me, drain_low, 0)
    lax.fori_loop(me + 1, n, drain_high, 0)


def local(query, key, value, grad_out, picks):
    n = lax.axis_size("ctx")
    me = lax.axis_index("ctx")
    targets = picks[:, :, 1:].reshape(TASKS * OTHERS)
    peers = jnp.arange(n, dtype=jnp.int32)
    named = (targets[None, :] == peers[:, None]) & (targets != me)[None, :]
    task = jnp.max(jnp.where(named, jnp.arange(TASKS * OTHERS, dtype=jnp.int32)[None, :], -1), axis=1)
    some = jnp.maximum(task, 0)
    tile_head = some // OTHERS
    width = max(n, TASKS * OTHERS)
    lists = [tile_head, jnp.where(task >= 0, tile_head % HEADS, -1), some, targets]
    table = jnp.stack([jnp.pad(r, (0, width - r.shape[0])) for r in lists])
    shape = jax.ShapeDtypeStruct((KEYS, COLS), bf16)

    def tiles(count, kind=bf16):
        return pltpu.VMEM((count, DIM, ROWS), kind)

    def rows(count, each=1):
        return pltpu.VMEM((count, each, ROWS), f32)

    vmem = pl.BlockSpec(memory_space=pltpu.VMEM)
    return pl.pallas_call(
        functools.partial(kernel, n),
        out_shape=[shape] * 4,
        in_specs=[pl.BlockSpec(memory_space=pltpu.SMEM)] + [vmem] * 4,
        out_specs=[vmem] * 4,
        scratch_shapes=[
            pltpu.VMEM((TASKS, DIM, ROWS), bf16),
            pltpu.VMEM((TASKS, DIM, ROWS), bf16),
            pltpu.VMEM((KEYS, COLS), bf16),
            pltpu.VMEM((COLS, KEYS), bf16),
            pltpu.VMEM((COLS, KEYS), bf16),
            pltpu.VMEM((n // 2 + TASKS // 2, KEYS, PAIR), bf16),
            tiles(n),
            tiles(n),
            rows(n),
            rows(n),
            tiles(n),
            tiles(n),
            rows(n, 2),
            rows(n, 2),
            tiles(TASKS * OTHERS),
            tiles(n),
            tiles(n),
            rows(TASKS * OTHERS),
            rows(n),
            rows(n),
            tiles(n),
            tiles(n),
            tiles(TASKS, f32),
            rows(TASKS, 2),
            tiles(TASKS),
            rows(TASKS),
            tiles(TASKS, f32),
            tiles(TASKS, f32),
            pltpu.VMEM((KEYS, COLS), f32),
            pltpu.VMEM((KEYS, COLS), f32),
            *[pltpu.SemaphoreType.DMA((n,))] * 8,
        ],
        compiler_params=pltpu.CompilerParams(
            collective_id=0, has_side_effects=True, vmem_limit_bytes=56 * 1024 * 1024
        ),
        name="block_sparse",
    )(table, query, key, value, grad_out)


def solution(mesh):
    whole = P("ctx", "head")
    return jax.shard_map(
        local,
        mesh=mesh,
        in_specs=(whole, whole, whole, whole, P("ctx", "head", None)),
        out_specs=(whole, whole, whole, whole),
        check_vma=False,
    )
```

time: 354 us -> 283 us (0.80)
  the two profiles are of different devices: /device:TPU:1 before, /device:TPU:15 now
where the time goes in v2:
time: 283 us; the launch traced here: 282 us
  Pallas kernels  276 us (98%)
  local copies, waits for them, and re-layouts  5.37 us (2%)
    pallas_call x1, Pallas kernels, local(): pl.pallas_call(functools.partial(kernel, n), out_shape=[shape] * 4, in_sp...  276 us

profile of v2, /device:TPU:15, one launch (start us, length us, event | category | flops | bytes accessed | tf_op | source)
XLA Modules:
  0.0 282.3 jit_solution(9884346334163543818)
XLA Ops:
  0.6 0.8 slice.3
  1.4 0.1 eq.17
  1.5 0.1 select_reduce_fusion
  1.7 0.6 pad_add_fusion.table
  2.2 275.5 %block_sparse.1 = (bf16[512,256]{1,0:T(8,128)(2,1)}, bf16[512,256]{1,0:T(8,128)(2,1)}, bf16[512,256]{1,0:T(8,128)(2,1)}, bf16[512,256]{1,0:T(8,128)(2,1)}) custom-call(s32[4,128]{1,0:T(4,128)} %pad_add_fusion.table, bf16[512,256]{1,0:T(8,128)(2,1)} %q_ref.1, bf16[512,256]{1,0:T(8,128)(2,1)} %k_ref.1, bf16[512,256]{1,0:T(8,128)(2,1)} %v_ref.1, ...), custom_call_target="tpu_custom_call" | custom-call | tf_op jit(solution)/shard_map/block_sparse/pallas_call | solution.py:376
  277.8 0.0 copy-start.2
  277.8 1.7 copy.13
  279.5 0.0 copy-done.2
  279.5 0.0 copy-start.1
  279.5 0.7 copy.14
  280.2 0.3 copy-done.1
  280.6 0.0 copy-start
  280.6 0.7 copy.15
  281.3 0.3 copy-done
  281.6 0.7 copy.16
  (3 shorter events, 0.0 us)
Async XLA Ops:
  277.8 1.7 copy-start.2
  279.5 1.0 copy-start.1
  280.6 1.0 copy-start

commit v3 on v2

--- a/solution.py
+++ b/solution.py
@@ -16,6 +16,7 @@
 COLS = HEADS * DIM
 PAIR = 2 * ROWS
 FAR = -1e30
+WINDOW = 24
 
 
 def dot(a, b):
@@ -41,12 +42,13 @@
     my_x, my_z, my_core = me // quarter, (me // 2) % depth, me % 2
 
     def along(i):
-        return jnp.where(i % 2 == 0, i // 2, depth - (i + 1) // 2)
-
-    def peer_of(i):
-        x = (my_x + 1 + i // quarter) % 4
-        z = (my_z + along((i // 2) % depth)) % depth
-        return x * quarter + z * 2 + (my_core + i) % 2
+        step = i // 2 + i % 2 * (depth // 2)
+        return jnp.where(i // 2 % 2 == 0, step, depth - step) % depth
+
+    def peer_of(m, core):
+        x = (my_x + 1 + m % 4) % 4
+        z = (my_z + along(m // 4)) % depth
+        return x * quarter + z * 2 + (my_core + core) % 2
 
     def source_pair(m):
         x = (my_x + 3 - m % 4) % 4
@@ -94,8 +96,8 @@
 
     pl.semaphore_wait(barrier, n - 1)
 
-    def send_tile(i, c):
-        d = peer_of(i)
+    def send_tile(m, core):
+        d = peer_of(m, core)
 
         @pl.when(d < me)
         def _():
@@ -103,10 +105,6 @@
             code_sent[d] = jnp.full((1, ROWS), table[1, d], jnp.int32).astype(f32)
             push(code_sent, code_got, send_c, recv_c, d)
             push(sent, got, send_a, recv_a, d)
-
-        return c
-
-    lax.fori_loop(0, n, send_tile, 0)
 
     def spread(x, mask):
         return jnp.concatenate([(x * mask[h : h + 1]).astype(bf16) for h in range(HEADS)], axis=0)
@@ -159,21 +157,17 @@
                 own_lse[a + i] = lse[:, i * ROWS : (i + 1) * ROWS]
         return c
 
-    lax.fori_loop(0, TILES, own_forward, 0)
-
     def masks(a, b):
         code = jnp.concatenate([code_got[a], code_got[b]], axis=1)
         row = lax.broadcasted_iota(jnp.int32, (8, PAIR), 0).astype(f32)
         return jnp.where(row == code, 1.0, 0.0)
 
-    def serve(m, c):
+    def serve(m):
         j = source_pair(m)
 
         @pl.when(j >= first)
         def _():
             serve_pair(j)
-
-        return c
 
     def serve_pair(j):
         a, b = 2 * j, 2 * j + 1
@@ -201,7 +195,23 @@
         push(lse_sent, lse_got, send_c, recv_c, b)
         push(back, ret, send_a, recv_a, b)
 
-    lax.fori_loop(0, last, serve, 0)
+    def tile_step(m, c):
+        @pl.when(m < last)
+        def _():
+            for core in range(2):
+                send_tile(m, core)
+
+        @pl.when(m == WINDOW - 1)
+        def _():
+            lax.fori_loop(0, TILES, own_forward, 0)
+
+        @pl.when(m >= WINDOW)
+        def _():
+            serve(m - WINDOW)
+
+        return c
+
+    lax.fori_loop(0, last + WINDOW, tile_step, 0)
 
     def wait_return(d, c):
         remote(lse_sent.at[d], lse_got.at[d], send_c, recv_c, d).wait_recv()
@@ -246,8 +256,8 @@
 
     lax.fori_loop(0, TASKS, combine, 0)
 
-    def send_grad(i, c):
-        d = peer_of(i)
+    def send_grad(m, core):
+        d = peer_of(m, core)
 
         @pl.when(d < me)
         def _():
@@ -256,13 +266,6 @@
             push(c_sent, c_got, send_d, recv_d, d)
             push(g_sent, g_got, send_b, recv_b, d)
 
-        return c
-
-    lax.fori_loop(0, n, send_grad, 0)
-
-    for t in range(TILES):
-        block = jnp.concatenate([attn[t * HEADS + h] for h in range(HEADS)], axis=0)
-        ao_ref[t * ROWS : (t + 1) * ROWS, :] = block.T.astype(bf16)
     dk_acc[...] = jnp.zeros_like(dk_acc)
     dv_acc[...] = jnp.zeros_like(dv_acc)
 
@@ -277,16 +280,12 @@
                 own_dq[a + i] = grad[:, i * ROWS : (i + 1) * ROWS]
         return c
 
-    lax.fori_loop(0, TILES, own_backward, 0)
-
-    def serve_back(m, c):
+    def serve_back(m):
         j = source_pair(m)
 
         @pl.when(j >= first)
         def _():
             serve_back_pair(j)
-
-        return c
 
     def serve_back_pair(j):
         a, b = 2 * j, 2 * j + 1
@@ -311,7 +310,26 @@
 
         push(dq_sent, dq_got, send_b, recv_b, b)
 
-    lax.fori_loop(0, last, serve_back, 0)
+    def grad_step(m, c):
+        @pl.when(m < last)
+        def _():
+            for core in range(2):
+                send_grad(m, core)
+
+        @pl.when(m == WINDOW - 1)
+        def _():
+            for t in range(TILES):
+                block = jnp.concatenate([attn[t * HEADS + h] for h in range(HEADS)], axis=0)
+                ao_ref[t * ROWS : (t + 1) * ROWS, :] = block.T.astype(bf16)
+            lax.fori_loop(0, TILES, own_backward, 0)
+
+        @pl.when(m >= WINDOW)
+        def _():
+            serve_back(m - WINDOW)
+
+        return c
+
+    lax.fori_loop(0, last + WINDOW, grad_step, 0)
     dk_ref[...] = (dk_acc[...] * 0.125).astype(bf16)
     dv_ref[...] = dv_acc[...].astype(bf16)
 

time: 283 us -> 270 us (0.954)
  the two profiles are of different devices: /device:TPU:15 before, /device:TPU:3 now
where the time goes in v3:
time: 270 us
  Pallas kernels  263 us (97%)
  local copies, waits for them, and re-layouts  5.37 us (2%)
    pallas_call x1, Pallas kernels, local(): pl.pallas_call(functools.partial(kernel, n), out_shape=[shape] * 4, in_sp...  263 us

profile of v3, /device:TPU:3, one launch (start us, length us, event | category | flops | bytes accessed | tf_op | source)
XLA Modules:
  0.0 269.7 jit_solution(17226868464210845222)
XLA Ops:
  0.6 0.8 slice.3
  1.4 0.1 eq.17
  1.5 0.1 select_reduce_fusion
  1.7 0.6 pad_add_fusion.table
  2.2 262.9 %block_sparse.1 = (bf16[512,256]{1,0:T(8,128)(2,1)}, bf16[512,256]{1,0:T(8,128)(2,1)}, bf16[512,256]{1,0:T(8,128)(2,1)}, bf16[512,256]{1,0:T(8,128)(2,1)}) custom-call(s32[4,128]{1,0:T(4,128)} %pad_add_fusion.table, bf16[512,256]{1,0:T(8,128)(2,1)} %q_ref.1, bf16[512,256]{1,0:T(8,128)(2,1)} %k_ref.1, bf16[512,256]{1,0:T(8,128)(2,1)} %v_ref.1, ...), custom_call_target="tpu_custom_call" | custom-call | tf_op jit(solution)/shard_map/block_sparse/pallas_call | solution.py:394
  265.2 0.0 copy-start.2
  265.2 1.7 copy.13
  266.9 0.0 copy-done.2
  266.9 0.0 copy-start.1
  266.9 0.7 copy.14
  267.6 0.3 copy-done.1
  268.0 0.0 copy-start
  268.0 0.7 copy.15
  268.7 0.3 copy-done
  269.0 0.7 copy.16
  (3 shorter events, 0.0 us)
Async XLA Ops:
  265.2 1.7 copy-start.2
  266.9 1.0 copy-start.1
  268.0 1.0 copy-start

commit v4 on v3

--- a/solution.py
+++ b/solution.py
@@ -16,7 +16,8 @@
 COLS = HEADS * DIM
 PAIR = 2 * ROWS
 FAR = -1e30
-WINDOW = 24
+LATE = 4
+WINDOW = 16
 
 
 def dot(a, b):
@@ -52,7 +53,9 @@
 
     def source_pair(m):
         x = (my_x + 3 - m % 4) % 4
-        return x * depth + (my_z + depth - along(m // 4)) % depth
+        zz = m // 4 - jnp.where(x == 3, LATE, 0)
+        j = x * depth + (my_z + 2 * depth - along(jnp.clip(zz, 0, depth - 1))) % depth
+        return j, (zz >= 0) & (zz < depth) & (j >= first)
 
     def remote(src, dst, send, recv, peer):
         return pltpu.make_async_remote_copy(
@@ -163,9 +166,9 @@
         return jnp.where(row == code, 1.0, 0.0)
 
     def serve(m):
-        j = source_pair(m)
-
-        @pl.when(j >= first)
+        j, live = source_pair(m)
+
+        @pl.when(live)
         def _():
             serve_pair(j)
 
@@ -211,7 +214,7 @@
 
         return c
 
-    lax.fori_loop(0, last + WINDOW, tile_step, 0)
+    lax.fori_loop(0, last + 4 * LATE + WINDOW, tile_step, 0)
 
     def wait_return(d, c):
         remote(lse_sent.at[d], lse_got.at[d], send_c, recv_c, d).wait_recv()
@@ -281,9 +284,9 @@
         return c
 
     def serve_back(m):
-        j = source_pair(m)
-
-        @pl.when(j >= first)
+        j, live = source_pair(m)
+
+        @pl.when(live)
         def _():
             serve_back_pair(j)
 
@@ -329,7 +332,7 @@
 
         return c
 
-    lax.fori_loop(0, last + WINDOW, grad_step, 0)
+    lax.fori_loop(0, last + 4 * LATE + WINDOW, grad_step, 0)
     dk_ref[...] = (dk_acc[...] * 0.125).astype(bf16)
     dv_ref[...] = dv_acc[...].astype(bf16)
 

time: 270 us -> 257 us (0.952)
  the two profiles are of different devices: /device:TPU:3 before, /device:TPU:39 now
where the time goes in v4:
time: 257 us
  Pallas kernels  250 us (97%)
  local copies, waits for them, and re-layouts  5.37 us (2%)
    pallas_call x1, Pallas kernels, local(): pl.pallas_call(functools.partial(kernel, n), out_shape=[shape] * 4, in_sp...  250 us

profile of v4, /device:TPU:39, one launch (start us, length us, event | category | flops | bytes accessed | tf_op | source)
XLA Modules:
  0.0 256.9 jit_solution(12251180457763186190)
XLA Ops:
  0.6 0.8 slice.3
  1.4 0.1 eq.17
  1.5 0.1 select_reduce_fusion
  1.7 0.6 pad_add_fusion.table
  2.2 250.1 %block_sparse.1 = (bf16[512,256]{1,0:T(8,128)(2,1)}, bf16[512,256]{1,0:T(8,128)(2,1)}, bf16[512,256]{1,0:T(8,128)(2,1)}, bf16[512,256]{1,0:T(8,128)(2,1)}) custom-call(s32[4,128]{1,0:T(4,128)} %pad_add_fusion.table, bf16[512,256]{1,0:T(8,128)(2,1)} %q_ref.1, bf16[512,256]{1,0:T(8,128)(2,1)} %k_ref.1, bf16[512,256]{1,0:T(8,128)(2,1)} %v_ref.1, ...), custom_call_target="tpu_custom_call" | custom-call | tf_op jit(solution)/shard_map/block_sparse/pallas_call | solution.py:397
  252.4 0.0 copy-start.2
  252.4 1.7 copy.13
  254.1 0.0 copy-done.2
  254.1 0.0 copy-start.1
  254.1 0.7 copy.14
  254.8 0.3 copy-done.1
  255.1 0.0 copy-start
  255.1 0.7 copy.15
  255.8 0.3 copy-done
  256.2 0.7 copy.16
  (3 shorter events, 0.0 us)
Async XLA Ops:
  252.4 1.7 copy-start.2
  254.1 1.0 copy-start.1
  255.1 1.0 copy-start
